TPU v7x, 32 devices: a whole 2x2x4 slice. The times are simulated.
32 devices in a mesh: gx: 8 (over z, core), gy: 4 (over y, x).
Axes of the slice: x: 2, y: 2, z: 4, core: 2. Of those that a mesh axis runs over, the one named last changes fastest.
Arguments:
- field: float32 [256, 128, 256], P('gx', 'gy'), may hold values from -192 to 192
- cond_x: float32 [256, 128, 256], P('gx', 'gy'), may hold values from 1 to 4
- cond_y: float32 [256, 128, 256], P('gx', 'gy'), may hold values from 1 to 4
- cross_weight: float32 [256, 128, 256], P('gx', 'gy'), may hold values from -4 to 4
Outputs:
- field_next: float32 [256, 128, 256], P('gx', 'gy')
All inputs are finite; a program needn't handle non-finite values.
Results may differ from a plain program's by a relative error of at most 0.0007.
Values sent between devices are 32-bit elements; how exact they have to be, the bound alone decides.
A program may use at most 64 MiB of HBM per device.

v0:
```python
import functools
import jax
import jax.numpy as jnp
from jax import lax
from jax.sharding import PartitionSpec as P
from jax.experimental import pallas as pl
from jax.experimental.pallas import tpu as pltpu

step_dt = 16384.0
LANES = 128
ROWS = 8
MESH = pl.DeviceIdType.MESH


def split_tiles(tiles, count):
    per_owner = next(p for p in range(1, tiles + 1) if tiles % p == 0 and p * count >= tiles)
    return per_owner, tiles // per_owner


class Sweep:
    def __init__(self, axis, count, tiles, refs):
        self.axis, self.count, self.tiles = axis, count, tiles
        self.per, self.owners = split_tiles(tiles, count)
        (self.t, self.rt, self.b, self.rb, self.s, self.rs, self.pe, self.sems) = refs
        self.me = lax.axis_index(axis)

    def others(self):
        return [lax.rem(self.me + d, self.count) for d in range(1, self.count)]

    def own(self):
        return pl.ds(self.me * self.per, self.per)

    def guarded(self, index, body):
        if self.owners == self.count:
            body()
        else:
            pl.when(index < self.owners)(body)

    def copy(self, kind, src, dst, target, sender):
        return pltpu.make_async_remote_copy(
            src_ref=src,
            dst_ref=dst,
            send_sem=self.sems.at[2 * kind, target],
            recv_sem=self.sems.at[2 * kind + 1, sender],
            device_id={self.axis: target},
            device_id_type=MESH,
        )

    def up(self, kind, target):
        mine, there = ((self.t, self.rt), (self.b, self.rb))[kind]
        return self.copy(kind, mine.at[pl.ds(target * self.per, self.per)], there.at[self.me], target, self.me)

    def up_from(self, kind, sender):
        mine, there = ((self.t, self.rt), (self.b, self.rb))[kind]
        return self.copy(kind, mine.at[pl.ds(0, self.per)], there.at[sender], sender, sender)

    def send(self, kind):
        for target in self.others():
            self.guarded(target, lambda target=target: self.up(kind, target).start())

        def keep():
            mine, there = ((self.t, self.rt), (self.b, self.rb))[kind]
            there[self.me] = mine[self.own()]

        self.guarded(self.me, keep)

    def prepare(self):
        def body():
            for sender in self.others():
                self.up_from(0, sender).wait_recv()
            shape = (self.per, ROWS, LANES)
            resistance = jnp.zeros(shape, jnp.float32)
            for j in range(self.count):
                inverse = 1.0 / (self.rt[j, :, 2] * resistance + self.rt[j, :, 3])
                self.pe[j, :, 0] = resistance
                self.pe[j, :, 1] = inverse
                resistance = (self.rt[j, :, 0] * resistance + self.rt[j, :, 1]) * inverse
            self.pe[self.count, :, 0] = resistance

        self.guarded(self.me, body)

    def back(self, target):
        return self.copy(2, self.s.at[target], self.rs.at[self.own()], target, self.me)

    def back_from(self, owner):
        return self.copy(2, self.s.at[owner], self.rs.at[pl.ds(owner * self.per, self.per)], owner, owner)

    def solve(self):
        def body():
            for sender in self.others():
                self.up_from(1, sender).wait_recv()
            shape = (self.per, ROWS, LANES)
            offset = jnp.zeros(shape, jnp.float32)
            offsets = []
            for j in range(self.count):
                offsets.append(offset)
                offset = offset * self.pe[j, :, 1] + self.rb[j, :, 0] - self.pe[j + 1, :, 0] * self.rb[j, :, 1]
            flux = jnp.zeros(shape, jnp.float32)
            for j in reversed(range(self.count)):
                flux = (flux - self.rt[j, :, 2] * offsets[j] - self.rb[j, :, 1]) * self.pe[j, :, 1]
                self.s[j, :, 0] = self.pe[j, :, 0] * flux + offsets[j]
                self.s[j, :, 1] = flux
            for target in self.others():
                self.back(target).start()
            self.rs[self.own()] = self.s[self.me]

        self.guarded(self.me, body)

    def receive(self):
        for d in range(1, self.count):
            owner = lax.rem(self.me + d, self.count)
            self.guarded(owner, lambda owner=owner: self.back_from(owner).wait_recv())

    def drain(self):
        def returned():
            for target in self.others():
                self.back(target).wait_send()

        for target in self.others():
            for kind in (0, 1):
                self.guarded(target, lambda target=target, kind=kind: self.up(kind, target).wait_send())
        self.guarded(self.me, returned)


def kernel(nx, ny, lx, ly, nh, *refs):
    field, cond_x, cond_y, weight, out = refs[:5]
    F, KX, KY, R, RY, HALF, HT, O, xh, ys, yh, ch, dl = refs[5:18]
    in_sem, out_sem, halo_send, halo_recv = refs[18:22]
    x_refs, y_refs = refs[22:30], refs[30:38]
    rtx, rty = ly // ROWS, lx // ROWS
    mx, my = lax.axis_index("gx"), lax.axis_index("gy")
    X = Sweep("gx", nx, nh * rtx, x_refs)
    Y = Sweep("gy", ny, nh * rty, y_refs)

    around = [(-1, 0), (1, 0), (0, -1), (0, 1), (-1, -1), (-1, 1), (1, -1), (1, 1)]

    def exists(dx, dy):
        there = None
        for d, m, n in ((dx, mx, nx), (dy, my, ny)):
            if d:
                ok = (m > 0) if d < 0 else (m < n - 1)
                there = ok if there is None else jnp.logical_and(there, ok)
        return there

    barrier = pltpu.get_barrier_semaphore()
    for target in X.others():
        pl.semaphore_signal(barrier, inc=1, device_id={"gx": target}, device_id_type=MESH)
    for target in Y.others():
        pl.semaphore_signal(barrier, inc=1, device_id={"gy": target}, device_id_type=MESH)
    for dx, dy in around[4:]:
        @pl.when(exists(dx, dy))
        def _(dx=dx, dy=dy):
            pl.semaphore_signal(barrier, inc=1, device_id={"gx": mx + dx, "gy": my + dy}, device_id_type=MESH)

    def lanes(h):
        return pl.ds(h * LANES, LANES)

    def load(k, h):
        src, dst = (
            (field, F.at[h, pl.ds(ly, lx * ly)]), (cond_x, KX.at[h]), (cond_y, KY.at[h]), (weight, R.at[h])
        )[k]
        return pltpu.make_async_copy(src.at[:, lanes(h)], dst, in_sem.at[k, h])

    for k in range(4):
        for h in range(nh):
            load(k, h).start()

    for h in range(nh):
        load(0, h).wait()
    for h in range(nh):
        ys[0, h] = F[h, pl.ds(ly, lx, stride=ly), :]
        ys[1, h] = F[h, pl.ds(ly + ly - 1, lx, stride=ly), :]

    def halo(k):
        dx, dy = around[k]
        if dy == 0:
            src = F.at[:, pl.ds(ly if dx < 0 else lx * ly, ly), :]
            dst = xh.at[1 if dx < 0 else 0]
        elif dx == 0:
            src = ys.at[0 if dy < 0 else 1]
            dst = yh.at[1 if dy < 0 else 0]
        else:
            src = ys.at[0 if dy < 0 else 1, :, pl.ds(0 if dx < 0 else lx - ROWS, ROWS), :]
            dst = ch.at[2 * (1 if dy < 0 else 0) + (1 if dx < 0 else 0)]
        return pltpu.make_async_remote_copy(
            src_ref=src,
            dst_ref=dst,
            send_sem=halo_send.at[k],
            recv_sem=halo_recv.at[around.index((-dx, -dy))],
            device_id={"gx": mx + dx, "gy": my + dy},
            device_id_type=MESH,
        )

    def halo_in(k):
        dx, dy = around[k]
        if dy == 0:
            dst = xh.at[0 if dx < 0 else 1]
        elif dx == 0:
            dst = yh.at[0 if dy < 0 else 1]
        else:
            dst = ch.at[2 * (0 if dy < 0 else 1) + (0 if dx < 0 else 1)]
        return dst, lambda: pltpu.make_async_remote_copy(
            src_ref=dst,
            dst_ref=dst,
            send_sem=halo_send.at[k],
            recv_sem=halo_recv.at[k],
            device_id={"gx": mx + dx, "gy": my + dy},
            device_id_type=MESH,
        )

    diagonal = sum(jnp.where(exists(dx, dy), 1, 0) for dx, dy in around[4:])
    pl.semaphore_wait(barrier, nx - 1 + ny - 1 + diagonal)

    for k, (dx, dy) in enumerate(around):
        @pl.when(exists(dx, dy))
        def _(k=k):
            halo(k).start()

    def rows(i, n):
        return pl.ds(pl.multiple_of(i * n, n), n)

    def put_tiles(ref, h, per_plane, values):
        for c, value in enumerate(values):
            for t in range(per_plane):
                ref[h * per_plane + t, c] = value[t * ROWS:(t + 1) * ROWS]

    def get_tiles(ref, h, per_plane, c):
        return jnp.concatenate([ref[h * per_plane + t, c] for t in range(per_plane)], axis=0)

    for k in (1,):
        for h in range(nh):
            load(k, h).wait()

    def transfer(length, width, resistance_at):
        def steps(g, carry):
            x0, j0, x1, j1 = carry
            for r in range(ROWS):
                rho = resistance_at(g * ROWS + r)
                x0 = x0 + rho * j0
                x1 = x1 + rho * j1
                j0 = j0 + x0
                j1 = j1 + x1
            return x0, j0, x1, j1

        zero = jnp.zeros((width, LANES), jnp.float32)
        one = jnp.ones((width, LANES), jnp.float32)
        x0, j0, x1, j1 = lax.fori_loop(0, length // ROWS, steps, (one, zero, zero, one))
        return x0, x1, j0, j1

    for h in range(nh):
        def resistance_x(i, h=h):
            rho = (1.0 / step_dt) / KX[h, rows(i, ly), :]
            KX[h, rows(i, ly), :] = rho
            return rho

        put_tiles(X.t, h, rtx, transfer(lx, ly, resistance_x))
    X.send(0)

    for h in range(nh):
        load(3, h).wait()
    for k, (dx, dy) in enumerate(around):
        @pl.when(exists(dx, dy))
        def _(k=k):
            halo_in(k)[1]().wait_recv()

        @pl.when(jnp.logical_not(exists(dx, dy)))
        def _(k=k):
            dst = halo_in(k)[0]
            dst[...] = jnp.zeros(dst.shape, jnp.float32)

    for h in range(nh):
        F[h, pl.ds(0, ly), :] = xh[0, h]
        F[h, pl.ds((lx + 1) * ly, ly), :] = xh[1, h]
        for side in range(2):
            edge = yh[side, h]
            before = jnp.concatenate([ch[2 * side, h, ROWS - 1:, :], edge[:-1]], axis=0)
            after = jnp.concatenate([edge[1:], ch[2 * side + 1, h, :1, :]], axis=0)
            dl[side, h] = after - before

    row = lax.broadcasted_iota(jnp.int32, (ly, LANES), 0)
    for h in range(nh):
        def steps(g, carry, h=h):
            x, j = carry
            low = dl[0, h, rows(g, ROWS), :]
            high = dl[1, h, rows(g, ROWS), :]
            for r in range(ROWS):
                i = g * ROWS + r
                across = F[h, rows(i + 2, ly), :] - F[h, rows(i, ly), :]
                above = jnp.where(row == ly - 1, high[r:r + 1], pltpu.roll(across, ly - 1, 0))
                below = jnp.where(row == 0, low[r:r + 1], pltpu.roll(across, 1, 0))
                source = F[h, rows(i + 1, ly), :] + R[h, rows(i, ly), :] * (above - below) * 0.25
                R[h, rows(i, ly), :] = source
                x = x + KX[h, rows(i, ly), :] * j
                j = j + (x - source)
            return x, j

        zero = jnp.zeros((ly, LANES), jnp.float32)
        put_tiles(X.b, h, rtx, lax.fori_loop(0, lx // ROWS, steps, (zero, zero)))
    X.send(1)

    for h in range(nh):
        load(2, h).wait()
    for h in range(nh):
        def resistance_y(i, h=h):
            rho = (1.0 / step_dt) / KY[h, pl.ds(i, lx, stride=ly), :]
            RY[h, rows(i, lx), :] = rho
            return rho

        put_tiles(Y.t, h, rty, transfer(ly, lx, resistance_y))
    Y.send(0)

    X.prepare()
    X.solve()
    Y.prepare()
    X.receive()

    for h in range(nh):
        def steps(g, carry, h=h):
            x, j = carry
            for r in range(ROWS):
                i = g * ROWS + r
                x = x + KX[h, rows(i, ly), :] * j
                j = j + (x - R[h, rows(i, ly), :])
                HALF[h, rows(i, ly), :] = x
            return x, j

        start = (get_tiles(X.rs, h, rtx, 0), get_tiles(X.rs, h, rtx, 1))
        lax.fori_loop(0, lx // ROWS, steps, start)

        def steps_y(g, carry, h=h):
            x, j = carry
            for r in range(ROWS):
                i = g * ROWS + r
                half = HALF[h, pl.ds(i, lx, stride=ly), :]
                HT[h, rows(i, lx), :] = half
                x = x + RY[h, rows(i, lx), :] * j
                j = j + (x - half)
            return x, j

        zero = jnp.zeros((lx, LANES), jnp.float32)
        put_tiles(Y.b, h, rty, lax.fori_loop(0, ly // ROWS, steps_y, (zero, zero)))
    Y.send(1)
    Y.solve()
    Y.receive()

    def store(h):
        return pltpu.make_async_copy(O.at[h], out.at[:, lanes(h)], out_sem.at[h])

    for h in range(nh):
        def steps(g, carry, h=h):
            x, j = carry
            for r in range(ROWS):
                i = g * ROWS + r
                x = x + RY[h, rows(i, lx), :] * j
                j = j + (x - HT[h, rows(i, lx), :])
                O[h, pl.ds(i, lx, stride=ly), :] = x
            return x, j

        start = (get_tiles(Y.rs, h, rty, 0), get_tiles(Y.rs, h, rty, 1))
        lax.fori_loop(0, ly // ROWS, steps, start)
        store(h).start()

    for k, (dx, dy) in enumerate(around):
        @pl.when(exists(dx, dy))
        def _(k=k):
            halo(k).wait_send()
    X.drain()
    Y.drain()
    for h in range(nh):
        store(h).wait()


def sweep_scratch(count, tiles):
    per, owners = split_tiles(tiles, count)
    return [
        pltpu.VMEM((tiles, 4, ROWS, LANES), jnp.float32),
        pltpu.VMEM((count, per, 4, ROWS, LANES), jnp.float32),
        pltpu.VMEM((tiles, 2, ROWS, LANES), jnp.float32),
        pltpu.VMEM((count, per, 2, ROWS, LANES), jnp.float32),
        pltpu.VMEM((count, per, 2, ROWS, LANES), jnp.float32),
        pltpu.VMEM((tiles, 2, ROWS, LANES), jnp.float32),
        pltpu.VMEM((count + 1, per, 2, ROWS, LANES), jnp.float32),
        pltpu.SemaphoreType.DMA((6, count)),
    ]


def shards(nx, ny, field, cond_x, cond_y, cross_weight):
    lx, ly, nz = field.shape
    nh = nz // LANES
    cells = (nh, lx * ly, LANES)
    flat = [a.reshape(lx * ly, nz) for a in (field, cond_x, cond_y, cross_weight)]
    scratch = [
        pltpu.VMEM((nh, (lx + 2) * ly, LANES), jnp.float32),
        *[pltpu.VMEM(cells, jnp.float32)] * 7,
        pltpu.VMEM((2, nh, ly, LANES), jnp.float32),
        pltpu.VMEM((2, nh, lx, LANES), jnp.float32),
        pltpu.VMEM((2, nh, lx, LANES), jnp.float32),
        pltpu.VMEM((4, nh, ROWS, LANES), jnp.float32),
        pltpu.VMEM((2, nh, lx, LANES), jnp.float32),
        pltpu.SemaphoreType.DMA((4, nh)),
        pltpu.SemaphoreType.DMA((nh,)),
        pltpu.SemaphoreType.DMA((8,)),
        pltpu.SemaphoreType.DMA((8,)),
        *sweep_scratch(nx, nh * ly // ROWS),
        *sweep_scratch(ny, nh * lx // ROWS),
    ]
    result = pl.pallas_call(
        functools.partial(kernel, nx, ny, lx, ly, nh),
        out_shape=jax.ShapeDtypeStruct((lx * ly, nz), jnp.float32),
        in_specs=[pl.BlockSpec(memory_space=pl.ANY)] * 4,
        out_specs=pl.BlockSpec(memory_space=pl.ANY),
        scratch_shapes=scratch,
        compiler_params=pltpu.CompilerParams(
            collective_id=0, has_side_effects=True, vmem_limit_bytes=40 * 1024 * 1024
        ),
        cost_estimate=pl.CostEstimate(
            flops=60 * lx * ly * nz, bytes_accessed=20 * lx * ly * nz, transcendentals=0
        ),
        name="adi_step",
    )(*flat)
    return result.reshape(lx, ly, nz)


def solution(mesh):
    spec = P("gx", "gy", None)
    return jax.shard_map(
        functools.partial(shards, mesh.shape["gx"], mesh.shape["gy"]),
        mesh=mesh,
        in_specs=(spec,) * 4,
        out_specs=spec,
        check_vma=False,
    )
```

profile of v0, /device:TPU:0, one launch (start us, length us, event | category | flops | bytes accessed | tf_op | source)
XLA Modules:
  0.0 33.2 jit_solution(6587026407059523779)
XLA Ops:
  0.0 0.0 copy-start
  0.0 1.2 %copy-done = f32[32,32,256]{2,1,0:T(8,128)S(1)} copy-done((f32[32,32,256]{2,1,0:T(8,128)S(1)}, f32[32,32,256]{2,1,0:T(8,128)}, u32[]{:S(2)}) %copy-start) | copy-done | bytes 1048600
  1.2 0.0 copy-start.1
  1.2 1.2 %copy-done.1 = f32[32,32,256]{2,1,0:T(8,128)S(1)} copy-done((f32[32,32,256]{2,1,0:T(8,128)S(1)}, f32[32,32,256]{2,1,0:T(8,128)}, u32[]{:S(2)}) %copy-start.1) | copy-done | bytes 1048600
  2.5 0.0 copy-start.2
  2.5 1.2 %copy-done.2 = f32[32,32,256]{2,1,0:T(8,128)S(1)} copy-done((f32[32,32,256]{2,1,0:T(8,128)S(1)}, f32[32,32,256]{2,1,0:T(8,128)}, u32[]{:S(2)}) %copy-start.2) | copy-done | bytes 1048600
  3.7 0.0 copy-start.3
  3.7 1.2 %copy-done.3 = f32[32,32,256]{2,1,0:T(8,128)S(1)} copy-done((f32[32,32,256]{2,1,0:T(8,128)S(1)}, f32[32,32,256]{2,1,0:T(8,128)}, u32[]{:S(2)}) %copy-start.3) | copy-done | bytes 1048600
  4.9 27.3 %adi_step.1 = f32[1024,256]{1,0:T(8,128)S(1)} custom-call(f32[1024,256]{1,0:T(8,128)S(1)} %bitcast.6, f32[1024,256]{1,0:T(8,128)S(1)} %bitcast.7, f32[1024,256]{1,0:T(8,128)S(1)} %bitcast.8, f32[1024,256]{1,0:T(8,128)S(1)} %bitcast.9), custom_call_target="tpu_custom_call" | custom-call | flops 15728640 | bytes 5242880 | tf_op jit(solution)/shard_map/adi_step/pallas_call | solution.py:407
  32.2 1.0 %copy.6 = f32[32,32,256]{2,1,0:T(8,128)} copy(f32[32,32,256]{2,1,0:T(8,128)S(1)} %bitcast.5) | data formatting | bytes 2097152
Async XLA Ops:
  0.0 1.2 %copy-start = (f32[32,32,256]{2,1,0:T(8,128)S(1)}, f32[32,32,256]{2,1,0:T(8,128)}, u32[]{:S(2)}) copy-start(f32[32,32,256]{2,1,0:T(8,128)} %param.4) | copy-start | bytes 3145732
  1.2 1.2 %copy-start.1 = (f32[32,32,256]{2,1,0:T(8,128)S(1)}, f32[32,32,256]{2,1,0:T(8,128)}, u32[]{:S(2)}) copy-start(f32[32,32,256]{2,1,0:T(8,128)} %param.5) | copy-start | bytes 3145732
  2.5 1.2 %copy-start.2 = (f32[32,32,256]{2,1,0:T(8,128)S(1)}, f32[32,32,256]{2,1,0:T(8,128)}, u32[]{:S(2)}) copy-start(f32[32,32,256]{2,1,0:T(8,128)} %param.6) | copy-start | bytes 3145732
  3.7 1.2 %copy-start.3 = (f32[32,32,256]{2,1,0:T(8,128)S(1)}, f32[32,32,256]{2,1,0:T(8,128)}, u32[]{:S(2)}) copy-start(f32[32,32,256]{2,1,0:T(8,128)} %param.7) | copy-start | bytes 3145732
where the time goes:
time: 33.5 us; the launch traced here: 33.2 us
  Pallas kernels  27.3 us (81%)
  local copies, waits for them, and re-layouts  5.87 us (18%)
    pallas_call x1, Pallas kernels, shards(): pl.pallas_call(functools.partial(kernel, nx, ny, lx, ly, nh), out_shape=j...  27.3 us
    unnamed x9, local copies, waits for them, and re-layouts  5.87 us

commit v1 on v0

--- a/solution.py
+++ b/solution.py
@@ -54,15 +54,22 @@
         mine, there = ((self.t, self.rt), (self.b, self.rb))[kind]
         return self.copy(kind, mine.at[pl.ds(0, self.per)], there.at[sender], sender, sender)
 
-    def send(self, kind):
-        for target in self.others():
-            self.guarded(target, lambda target=target: self.up(kind, target).start())
+    def send(self, kind, part=0, parts=1):
+        low, high = self.owners * part // parts, self.owners * (part + 1) // parts
+
+        def inside(index, body):
+            if parts == 1:
+                self.guarded(index, body)
+            else:
+                pl.when(jnp.logical_and(index >= low, index < high))(body)
 
         def keep():
             mine, there = ((self.t, self.rt), (self.b, self.rb))[kind]
             there[self.me] = mine[self.own()]
 
-        self.guarded(self.me, keep)
+        for target in self.others():
+            inside(target, lambda target=target: self.up(kind, target).start())
+        inside(self.me, keep)
 
     def prepare(self):
         def body():
@@ -106,10 +113,10 @@
 
         self.guarded(self.me, body)
 
-    def receive(self):
-        for d in range(1, self.count):
-            owner = lax.rem(self.me + d, self.count)
-            self.guarded(owner, lambda owner=owner: self.back_from(owner).wait_recv())
+    def receive(self, part, parts):
+        low, high = self.owners * part // parts, self.owners * (part + 1) // parts
+        for owner in range(low, high):
+            pl.when(self.me != owner)(lambda owner=owner: self.back_from(owner).wait_recv())
 
     def drain(self):
         def returned():
@@ -123,10 +130,11 @@
 
 
 def kernel(nx, ny, lx, ly, nh, *refs):
-    field, cond_x, cond_y, weight, out = refs[:5]
-    F, KX, KY, R, RY, HALF, HT, O, xh, ys, yh, ch, dl = refs[5:18]
-    in_sem, out_sem, halo_send, halo_recv = refs[18:22]
-    x_refs, y_refs = refs[22:30], refs[30:38]
+    field, cond_x, cond_y, weight = refs[:4]
+    out, refs = refs[4:4 + nh], refs[4 + nh - 5:]
+    F, KX, KY, R, RY, HALF, HT, xh, ys, yh, ch, dl = refs[5:17]
+    in_sem, halo_send, halo_recv = refs[17:20]
+    x_refs, y_refs = refs[20:28], refs[28:36]
     rtx, rty = ly // ROWS, lx // ROWS
     mx, my = lax.axis_index("gx"), lax.axis_index("gy")
     X = Sweep("gx", nx, nh * rtx, x_refs)
@@ -227,6 +235,18 @@
     def get_tiles(ref, h, per_plane, c):
         return jnp.concatenate([ref[h * per_plane + t, c] for t in range(per_plane)], axis=0)
 
+    def send_part(sweep, h):
+        if sweep.owners % nh == 0:
+            sweep.send(1, h, nh)
+        elif h == nh - 1:
+            sweep.send(1)
+
+    def receive_part(sweep, h):
+        if sweep.owners % nh == 0:
+            sweep.receive(h, nh)
+        elif h == 0:
+            sweep.receive(0, 1)
+
     for k in (1,):
         for h in range(nh):
             load(k, h).wait()
@@ -296,7 +316,8 @@
 
         zero = jnp.zeros((ly, LANES), jnp.float32)
         put_tiles(X.b, h, rtx, lax.fori_loop(0, lx // ROWS, steps, (zero, zero)))
-    X.send(1)
+        send_part(X, h)
+    X.prepare()
 
     for h in range(nh):
         load(2, h).wait()
@@ -309,12 +330,12 @@
         put_tiles(Y.t, h, rty, transfer(ly, lx, resistance_y))
     Y.send(0)
 
-    X.prepare()
     X.solve()
     Y.prepare()
-    X.receive()
-
-    for h in range(nh):
+
+    for h in range(nh):
+        receive_part(X, h)
+
         def steps(g, carry, h=h):
             x, j = carry
             for r in range(ROWS):
@@ -339,35 +360,31 @@
 
         zero = jnp.zeros((lx, LANES), jnp.float32)
         put_tiles(Y.b, h, rty, lax.fori_loop(0, ly // ROWS, steps_y, (zero, zero)))
-    Y.send(1)
+        send_part(Y, h)
+
+    for k, (dx, dy) in enumerate(around):
+        @pl.when(exists(dx, dy))
+        def _(k=k):
+            halo(k).wait_send()
+    X.drain()
     Y.solve()
-    Y.receive()
-
-    def store(h):
-        return pltpu.make_async_copy(O.at[h], out.at[:, lanes(h)], out_sem.at[h])
-
-    for h in range(nh):
+
+    for h in range(nh):
+        receive_part(Y, h)
+
         def steps(g, carry, h=h):
             x, j = carry
             for r in range(ROWS):
                 i = g * ROWS + r
                 x = x + RY[h, rows(i, lx), :] * j
                 j = j + (x - HT[h, rows(i, lx), :])
-                O[h, pl.ds(i, lx, stride=ly), :] = x
+                out[h][pl.ds(i, lx, stride=ly), :] = x
             return x, j
 
         start = (get_tiles(Y.rs, h, rty, 0), get_tiles(Y.rs, h, rty, 1))
         lax.fori_loop(0, ly // ROWS, steps, start)
-        store(h).start()
-
-    for k, (dx, dy) in enumerate(around):
-        @pl.when(exists(dx, dy))
-        def _(k=k):
-            halo(k).wait_send()
-    X.drain()
+
     Y.drain()
-    for h in range(nh):
-        store(h).wait()
 
 
 def sweep_scratch(count, tiles):
@@ -388,17 +405,19 @@
     lx, ly, nz = field.shape
     nh = nz // LANES
     cells = (nh, lx * ly, LANES)
-    flat = [a.reshape(lx * ly, nz) for a in (field, cond_x, cond_y, cross_weight)]
+    flat = [
+        pltpu.with_memory_space_constraint(a.reshape(lx * ly, nz), pltpu.HBM)
+        for a in (field, cond_x, cond_y, cross_weight)
+    ]
     scratch = [
         pltpu.VMEM((nh, (lx + 2) * ly, LANES), jnp.float32),
-        *[pltpu.VMEM(cells, jnp.float32)] * 7,
+        *[pltpu.VMEM(cells, jnp.float32)] * 6,
         pltpu.VMEM((2, nh, ly, LANES), jnp.float32),
         pltpu.VMEM((2, nh, lx, LANES), jnp.float32),
         pltpu.VMEM((2, nh, lx, LANES), jnp.float32),
         pltpu.VMEM((4, nh, ROWS, LANES), jnp.float32),
         pltpu.VMEM((2, nh, lx, LANES), jnp.float32),
         pltpu.SemaphoreType.DMA((4, nh)),
-        pltpu.SemaphoreType.DMA((nh,)),
         pltpu.SemaphoreType.DMA((8,)),
         pltpu.SemaphoreType.DMA((8,)),
         *sweep_scratch(nx, nh * ly // ROWS),
@@ -406,9 +425,9 @@
     ]
     result = pl.pallas_call(
         functools.partial(kernel, nx, ny, lx, ly, nh),
-        out_shape=jax.ShapeDtypeStruct((lx * ly, nz), jnp.float32),
-        in_specs=[pl.BlockSpec(memory_space=pl.ANY)] * 4,
-        out_specs=pl.BlockSpec(memory_space=pl.ANY),
+        out_shape=[pltpu.VMEM(cells[1:], jnp.float32)] * nh,
+        in_specs=[pl.BlockSpec(memory_space=pltpu.HBM)] * 4,
+        out_specs=[pl.BlockSpec(memory_space=pltpu.VMEM)] * nh,
         scratch_shapes=scratch,
         compiler_params=pltpu.CompilerParams(
             collective_id=0, has_side_effects=True, vmem_limit_bytes=40 * 1024 * 1024
@@ -418,7 +437,7 @@
         ),
         name="adi_step",
     )(*flat)
-    return result.reshape(lx, ly, nz)
+    return jnp.concatenate(result, axis=1).reshape(lx, ly, nz)
 
 
 def solution(mesh):

time: 33.5 us -> 26.8 us (0.80)
  local copies, waits for them, and re-layouts: 5.87 us -> 0 us
  Pallas kernels: 27.3 us -> 25.6 us
  other arithmetic: 0 us -> 1.04 us
    unnamed x9 -> x0, local copies, waits for them, and re-layouts: 5.87 us -> none
    pallas_call x1, Pallas kernels: 27.3 us -> 25.6 us  [shards(): pl.pallas_call(functools.partial(kernel, nx, ny, lx, ly, nh), out_shape=[...]
    concatenate x0 -> x1, other arithmetic: none -> 1.04 us  [shards(): return jnp.concatenate(result, axis=1).reshape(lx, ly, nz)]
where the time goes in v1:
time: 26.8 us; the launch traced here: 26.6 us
  Pallas kernels  25.6 us (96%)
  other arithmetic  1.04 us (4%)
    pallas_call x1, Pallas kernels, shards(): pl.pallas_call(functools.partial(kernel, nx, ny, lx, ly, nh), out_shape=[...  25.6 us
    concatenate x1, other arithmetic, shards(): return jnp.concatenate(result, axis=1).reshape(lx, ly, nz)  1.04 us

profile of v1, /device:TPU:0, one launch (start us, length us, event | category | flops | bytes accessed | tf_op | source)
XLA Modules:
  0.0 26.6 jit_solution(15399396763699318880)
XLA Ops:
  0.0 25.6 %adi_step.1 = (f32[1024,128]{1,0:T(8,128)S(1)}, f32[1024,128]{1,0:T(8,128)S(1)}) custom-call(f32[1024,256]{1,0:T(8,128)} %bitcast.5, f32[1024,256]{1,0:T(8,128)} %bitcast.6, f32[1024,256]{1,0:T(8,128)} %bitcast.7, f32[1024,256]{1,0:T(8,128)} %bitcast.8), custom_call_target="tpu_custom_call" | custom-call | flops 15728640 | bytes 5242880 | tf_op jit(solution)/shard_map/adi_step/pallas_call | solution.py:426
  25.6 1.0 %pad_maximum_fusion = f32[1024,256]{1,0:T(8,128)} fusion(f32[1024,128]{1,0:T(8,128)S(1)} %get-tuple-element.8, f32[1024,128]{1,0:T(8,128)S(1)} %get-tuple-element.7), kind=kLoop, calls=%fused_computation | loop fusion | flops 262144 | bytes 2097152 | tf_op jit(solution)/shard_map/concatenate | solution.py:440

commit v2 on v1

--- a/solution.py
+++ b/solution.py
@@ -18,10 +18,11 @@
 
 
 class Sweep:
-    def __init__(self, axis, count, tiles, refs):
+    def __init__(self, axis, count, tiles, parts, refs):
         self.axis, self.count, self.tiles = axis, count, tiles
         self.per, self.owners = split_tiles(tiles, count)
-        (self.t, self.rt, self.b, self.rb, self.s, self.rs, self.pe, self.sems) = refs
+        self.parts = parts if self.owners % parts == 0 else 1
+        (self.t, self.rt, self.b, self.rb, self.s, self.rs, self.pe, self.up_sems, self.back_sems) = refs
         self.me = lax.axis_index(axis)
 
     def others(self):
@@ -30,53 +31,60 @@
     def own(self):
         return pl.ds(self.me * self.per, self.per)
 
+    def bounds(self, part):
+        return self.owners * part // self.parts, self.owners * (part + 1) // self.parts
+
+    def within(self, index, low, high, body):
+        if low == 0 and high == self.count:
+            body()
+        elif low == 0:
+            pl.when(index < high)(body)
+        elif high == self.count:
+            pl.when(index >= low)(body)
+        else:
+            pl.when(jnp.logical_and(index >= low, index < high))(body)
+
     def guarded(self, index, body):
-        if self.owners == self.count:
-            body()
-        else:
-            pl.when(index < self.owners)(body)
-
-    def copy(self, kind, src, dst, target, sender):
+        self.within(index, 0, self.owners, body)
+
+    def copy(self, src, dst, send_sem, recv_sem, target):
         return pltpu.make_async_remote_copy(
             src_ref=src,
             dst_ref=dst,
-            send_sem=self.sems.at[2 * kind, target],
-            recv_sem=self.sems.at[2 * kind + 1, sender],
+            send_sem=send_sem,
+            recv_sem=recv_sem,
             device_id={self.axis: target},
             device_id_type=MESH,
         )
 
-    def up(self, kind, target):
-        mine, there = ((self.t, self.rt), (self.b, self.rb))[kind]
-        return self.copy(kind, mine.at[pl.ds(target * self.per, self.per)], there.at[self.me], target, self.me)
-
-    def up_from(self, kind, sender):
-        mine, there = ((self.t, self.rt), (self.b, self.rb))[kind]
-        return self.copy(kind, mine.at[pl.ds(0, self.per)], there.at[sender], sender, sender)
-
-    def send(self, kind, part=0, parts=1):
-        low, high = self.owners * part // parts, self.owners * (part + 1) // parts
-
-        def inside(index, body):
-            if parts == 1:
-                self.guarded(index, body)
-            else:
-                pl.when(jnp.logical_and(index >= low, index < high))(body)
+    def buffers(self, kind):
+        return ((self.t, self.rt), (self.b, self.rb))[kind]
+
+    def up(self, kind, src, dst, target):
+        return self.copy(src, dst, self.up_sems.at[kind, 0], self.up_sems.at[kind, 1], target)
+
+    def send(self, kind, part=None):
+        low, high = (0, self.owners) if part is None else self.bounds(part)
+        mine, there = self.buffers(kind)
+
+        def start(target):
+            self.up(kind, mine.at[pl.ds(target * self.per, self.per)], there.at[self.me], target).start()
 
         def keep():
-            mine, there = ((self.t, self.rt), (self.b, self.rb))[kind]
             there[self.me] = mine[self.own()]
 
         for target in self.others():
-            inside(target, lambda target=target: self.up(kind, target).start())
-        inside(self.me, keep)
+            self.within(target, low, high, lambda target=target: start(target))
+        self.within(self.me, low, high, keep)
+
+    def arrived(self, kind):
+        there = self.buffers(kind)[1].at[pl.ds(0, self.count - 1)]
+        self.up(kind, there, there, self.others()[0]).wait_recv()
 
     def prepare(self):
         def body():
-            for sender in self.others():
-                self.up_from(0, sender).wait_recv()
-            shape = (self.per, ROWS, LANES)
-            resistance = jnp.zeros(shape, jnp.float32)
+            self.arrived(0)
+            resistance = jnp.zeros((self.per, ROWS, LANES), jnp.float32)
             for j in range(self.count):
                 inverse = 1.0 / (self.rt[j, :, 2] * resistance + self.rt[j, :, 3])
                 self.pe[j, :, 0] = resistance
@@ -86,59 +94,72 @@
 
         self.guarded(self.me, body)
 
-    def back(self, target):
-        return self.copy(2, self.s.at[target], self.rs.at[self.own()], target, self.me)
-
-    def back_from(self, owner):
-        return self.copy(2, self.s.at[owner], self.rs.at[pl.ds(owner * self.per, self.per)], owner, owner)
+    def back(self, src, dst, part, target):
+        return self.copy(src, dst, self.back_sems.at[0], self.back_sems.at[1 + part], target)
 
     def solve(self):
+        part = lax.div(self.me, self.owners // self.parts)
+
         def body():
-            for sender in self.others():
-                self.up_from(1, sender).wait_recv()
-            shape = (self.per, ROWS, LANES)
-            offset = jnp.zeros(shape, jnp.float32)
+            self.arrived(1)
+            offset = jnp.zeros((self.per, ROWS, LANES), jnp.float32)
             offsets = []
             for j in range(self.count):
                 offsets.append(offset)
-                offset = offset * self.pe[j, :, 1] + self.rb[j, :, 0] - self.pe[j + 1, :, 0] * self.rb[j, :, 1]
-            flux = jnp.zeros(shape, jnp.float32)
+                offset = offset * self.pe[j, :, 1] + (self.rb[j, :, 0] - self.pe[j + 1, :, 0] * self.rb[j, :, 1])
+            flux = jnp.zeros((self.per, ROWS, LANES), jnp.float32)
             for j in reversed(range(self.count)):
-                flux = (flux - self.rt[j, :, 2] * offsets[j] - self.rb[j, :, 1]) * self.pe[j, :, 1]
+                share = (self.rt[j, :, 2] * offsets[j] + self.rb[j, :, 1]) * self.pe[j, :, 1]
+                flux = flux * self.pe[j, :, 1] - share
                 self.s[j, :, 0] = self.pe[j, :, 0] * flux + offsets[j]
                 self.s[j, :, 1] = flux
             for target in self.others():
-                self.back(target).start()
+                self.back(self.s.at[target], self.rs.at[self.own()], part, target).start()
             self.rs[self.own()] = self.s[self.me]
 
         self.guarded(self.me, body)
 
-    def receive(self, part, parts):
-        low, high = self.owners * part // parts, self.owners * (part + 1) // parts
-        for owner in range(low, high):
-            pl.when(self.me != owner)(lambda owner=owner: self.back_from(owner).wait_recv())
+    def receive(self, part):
+        if part >= self.parts:
+            return
+        low, high = self.bounds(part)
+
+        def wait(owners):
+            if owners:
+                there = self.rs.at[pl.ds(0, owners * self.per)]
+                self.back(there, there, part, self.others()[0]).wait_recv()
+
+        inside = jnp.logical_and(self.me >= low, self.me < high)
+        pl.when(inside)(lambda: wait(high - low - 1))
+        pl.when(jnp.logical_not(inside))(lambda: wait(high - low))
 
     def drain(self):
-        def returned():
-            for target in self.others():
-                self.back(target).wait_send()
-
-        for target in self.others():
+        def sent(owners):
             for kind in (0, 1):
-                self.guarded(target, lambda target=target, kind=kind: self.up(kind, target).wait_send())
-        self.guarded(self.me, returned)
-
-
-def kernel(nx, ny, lx, ly, nh, *refs):
+                if owners:
+                    mine = self.buffers(kind)[0].at[pl.ds(0, owners * self.per)]
+                    self.up(kind, mine, mine, self.others()[0]).wait_send()
+
+        def owner():
+            sent(self.owners - 1)
+            mine = self.s.at[pl.ds(0, self.count - 1)]
+            self.back(mine, mine, 0, self.others()[0]).wait_send()
+
+        self.guarded(self.me, owner)
+        if self.owners < self.count:
+            pl.when(self.me >= self.owners)(lambda: sent(self.owners))
+
+
+def kernel(nx, ny, lx, ly, nh, pitch, *refs):
     field, cond_x, cond_y, weight = refs[:4]
     out, refs = refs[4:4 + nh], refs[4 + nh - 5:]
     F, KX, KY, R, RY, HALF, HT, xh, ys, yh, ch, dl = refs[5:17]
     in_sem, halo_send, halo_recv = refs[17:20]
-    x_refs, y_refs = refs[20:28], refs[28:36]
+    x_refs, y_refs = refs[20:29], refs[29:38]
     rtx, rty = ly // ROWS, lx // ROWS
     mx, my = lax.axis_index("gx"), lax.axis_index("gy")
-    X = Sweep("gx", nx, nh * rtx, x_refs)
-    Y = Sweep("gy", ny, nh * rty, y_refs)
+    X = Sweep("gx", nx, nh * rtx, nh, x_refs)
+    Y = Sweep("gy", ny, nh * rty, nh, y_refs)
 
     around = [(-1, 0), (1, 0), (0, -1), (0, 1), (-1, -1), (-1, 1), (1, -1), (1, 1)]
 
@@ -169,12 +190,16 @@
         )[k]
         return pltpu.make_async_copy(src.at[:, lanes(h)], dst, in_sem.at[k, h])
 
-    for k in range(4):
+    def start(k):
         for h in range(nh):
             load(k, h).start()
 
+    start(0)
+    start(1)
+
     for h in range(nh):
         load(0, h).wait()
+    start(3)
     for h in range(nh):
         ys[0, h] = F[h, pl.ds(ly, lx, stride=ly), :]
         ys[1, h] = F[h, pl.ds(ly + ly - 1, lx, stride=ly), :]
@@ -224,6 +249,12 @@
         def _(k=k):
             halo(k).start()
 
+    for k, (dx, dy) in enumerate(around):
+        @pl.when(jnp.logical_not(exists(dx, dy)))
+        def _(k=k):
+            dst = halo_in(k)[0]
+            dst[...] = jnp.zeros(dst.shape, jnp.float32)
+
     def rows(i, n):
         return pl.ds(pl.multiple_of(i * n, n), n)
 
@@ -236,20 +267,10 @@
         return jnp.concatenate([ref[h * per_plane + t, c] for t in range(per_plane)], axis=0)
 
     def send_part(sweep, h):
-        if sweep.owners % nh == 0:
-            sweep.send(1, h, nh)
+        if sweep.parts == nh:
+            sweep.send(1, h)
         elif h == nh - 1:
             sweep.send(1)
-
-    def receive_part(sweep, h):
-        if sweep.owners % nh == 0:
-            sweep.receive(h, nh)
-        elif h == 0:
-            sweep.receive(0, 1)
-
-    for k in (1,):
-        for h in range(nh):
-            load(k, h).wait()
 
     def transfer(length, width, resistance_at):
         def steps(g, carry):
@@ -268,6 +289,10 @@
         return x0, x1, j0, j1
 
     for h in range(nh):
+        load(1, h).wait()
+        if h == nh - 1:
+            start(2)
+
         def resistance_x(i, h=h):
             rho = (1.0 / step_dt) / KX[h, rows(i, ly), :]
             KX[h, rows(i, ly), :] = rho
@@ -276,17 +301,10 @@
         put_tiles(X.t, h, rtx, transfer(lx, ly, resistance_x))
     X.send(0)
 
-    for h in range(nh):
-        load(3, h).wait()
     for k, (dx, dy) in enumerate(around):
         @pl.when(exists(dx, dy))
         def _(k=k):
             halo_in(k)[1]().wait_recv()
-
-        @pl.when(jnp.logical_not(exists(dx, dy)))
-        def _(k=k):
-            dst = halo_in(k)[0]
-            dst[...] = jnp.zeros(dst.shape, jnp.float32)
 
     for h in range(nh):
         F[h, pl.ds(0, ly), :] = xh[0, h]
@@ -299,6 +317,8 @@
 
     row = lax.broadcasted_iota(jnp.int32, (ly, LANES), 0)
     for h in range(nh):
+        load(3, h).wait()
+
         def steps(g, carry, h=h):
             x, j = carry
             low = dl[0, h, rows(g, ROWS), :]
@@ -311,7 +331,7 @@
                 source = F[h, rows(i + 1, ly), :] + R[h, rows(i, ly), :] * (above - below) * 0.25
                 R[h, rows(i, ly), :] = source
                 x = x + KX[h, rows(i, ly), :] * j
-                j = j + (x - source)
+                j = (j - source) + x
             return x, j
 
         zero = jnp.zeros((ly, LANES), jnp.float32)
@@ -321,7 +341,7 @@
 
     for h in range(nh):
         load(2, h).wait()
-    for h in range(nh):
+
         def resistance_y(i, h=h):
             rho = (1.0 / step_dt) / KY[h, pl.ds(i, lx, stride=ly), :]
             RY[h, rows(i, lx), :] = rho
@@ -334,15 +354,15 @@
     Y.prepare()
 
     for h in range(nh):
-        receive_part(X, h)
+        X.receive(h)
 
         def steps(g, carry, h=h):
             x, j = carry
             for r in range(ROWS):
                 i = g * ROWS + r
                 x = x + KX[h, rows(i, ly), :] * j
-                j = j + (x - R[h, rows(i, ly), :])
-                HALF[h, rows(i, ly), :] = x
+                j = (j - R[h, rows(i, ly), :]) + x
+                HALF[h, pl.ds(pl.multiple_of(i * pitch, ROWS), ly), :] = x
             return x, j
 
         start = (get_tiles(X.rs, h, rtx, 0), get_tiles(X.rs, h, rtx, 1))
@@ -352,10 +372,10 @@
             x, j = carry
             for r in range(ROWS):
                 i = g * ROWS + r
-                half = HALF[h, pl.ds(i, lx, stride=ly), :]
+                half = HALF[h, pl.ds(i, lx, stride=pitch), :]
                 HT[h, rows(i, lx), :] = half
                 x = x + RY[h, rows(i, lx), :] * j
-                j = j + (x - half)
+                j = (j - half) + x
             return x, j
 
         zero = jnp.zeros((lx, LANES), jnp.float32)
@@ -370,14 +390,14 @@
     Y.solve()
 
     for h in range(nh):
-        receive_part(Y, h)
+        Y.receive(h)
 
         def steps(g, carry, h=h):
             x, j = carry
             for r in range(ROWS):
                 i = g * ROWS + r
                 x = x + RY[h, rows(i, lx), :] * j
-                j = j + (x - HT[h, rows(i, lx), :])
+                j = (j - HT[h, rows(i, lx), :]) + x
                 out[h][pl.ds(i, lx, stride=ly), :] = x
             return x, j
 
@@ -387,7 +407,7 @@
     Y.drain()
 
 
-def sweep_scratch(count, tiles):
+def sweep_scratch(count, tiles, parts):
     per, owners = split_tiles(tiles, count)
     return [
         pltpu.VMEM((tiles, 4, ROWS, LANES), jnp.float32),
@@ -397,7 +417,8 @@
         pltpu.VMEM((count, per, 2, ROWS, LANES), jnp.float32),
         pltpu.VMEM((tiles, 2, ROWS, LANES), jnp.float32),
         pltpu.VMEM((count + 1, per, 2, ROWS, LANES), jnp.float32),
-        pltpu.SemaphoreType.DMA((6, count)),
+        pltpu.SemaphoreType.DMA((2, 2)),
+        pltpu.SemaphoreType.DMA((1 + parts,)),
     ]
 
 
@@ -405,13 +426,16 @@
     lx, ly, nz = field.shape
     nh = nz // LANES
     cells = (nh, lx * ly, LANES)
+    pitch = ly + ROWS if ly // ROWS % 2 == 0 else ly
     flat = [
         pltpu.with_memory_space_constraint(a.reshape(lx * ly, nz), pltpu.HBM)
         for a in (field, cond_x, cond_y, cross_weight)
     ]
     scratch = [
         pltpu.VMEM((nh, (lx + 2) * ly, LANES), jnp.float32),
-        *[pltpu.VMEM(cells, jnp.float32)] * 6,
+        *[pltpu.VMEM(cells, jnp.float32)] * 4,
+        pltpu.VMEM((nh, lx * pitch, LANES), jnp.float32),
+        pltpu.VMEM(cells, jnp.float32),
         pltpu.VMEM((2, nh, ly, LANES), jnp.float32),
         pltpu.VMEM((2, nh, lx, LANES), jnp.float32),
         pltpu.VMEM((2, nh, lx, LANES), jnp.float32),
@@ -420,12 +444,12 @@
         pltpu.SemaphoreType.DMA((4, nh)),
         pltpu.SemaphoreType.DMA((8,)),
         pltpu.SemaphoreType.DMA((8,)),
-        *sweep_scratch(nx, nh * ly // ROWS),
-        *sweep_scratch(ny, nh * lx // ROWS),
+        *sweep_scratch(nx, nh * ly // ROWS, nh),
+        *sweep_scratch(ny, nh * lx // ROWS, nh),
     ]
     result = pl.pallas_call(
-        functools.partial(kernel, nx, ny, lx, ly, nh),
-        out_shape=[pltpu.VMEM(cells[1:], jnp.float32)] * nh,
+        functools.partial(kernel, nx, ny, lx, ly, nh, pitch),
+        out_shape=[pltpu.VMEM((lx * ly, LANES), jnp.float32)] * nh,
         in_specs=[pl.BlockSpec(memory_space=pltpu.HBM)] * 4,
         out_specs=[pl.BlockSpec(memory_space=pltpu.VMEM)] * nh,
         scratch_shapes=scratch,
@@ -437,6 +461,7 @@
         ),
         name="adi_step",
     )(*flat)
+
     return jnp.concatenate(result, axis=1).reshape(lx, ly, nz)
 
 

time: 26.8 us -> 25.9 us (0.966)
  Pallas kernels: 25.6 us -> 24.8 us
    pallas_call x1, Pallas kernels: 25.6 us -> 24.8 us  [shards(): pl.pallas_call(functools.partial(kernel, nx, ny, lx, ly, nh, pitch), out_...]
where the time goes in v2:
time: 25.9 us; the launch traced here: 25.8 us
  Pallas kernels  24.8 us (96%)
  other arithmetic  1.04 us (4%)
    pallas_call x1, Pallas kernels, shards(): pl.pallas_call(functools.partial(kernel, nx, ny, lx, ly, nh, pitch), out_...  24.8 us
    concatenate x1, other arithmetic, shards(): return jnp.concatenate(result, axis=1).reshape(lx, ly, nz)  1.04 us

profile of v2, /device:TPU:0, one launch (start us, length us, event | category | flops | bytes accessed | tf_op | source)
XLA Modules:
  0.0 25.8 jit_solution(1538873922758333000)
XLA Ops:
  0.0 24.8 %adi_step.1 = (f32[1024,128]{1,0:T(8,128)S(1)}, f32[1024,128]{1,0:T(8,128)S(1)}) custom-call(f32[1024,256]{1,0:T(8,128)} %bitcast.5, f32[1024,256]{1,0:T(8,128)} %bitcast.6, f32[1024,256]{1,0:T(8,128)} %bitcast.7, f32[1024,256]{1,0:T(8,128)} %bitcast.8), custom_call_target="tpu_custom_call" | custom-call | flops 15728640 | bytes 5242880 | tf_op jit(solution)/shard_map/adi_step/pallas_call | solution.py:450
  24.8 1.0 %pad_maximum_fusion = f32[1024,256]{1,0:T(8,128)} fusion(f32[1024,128]{1,0:T(8,128)S(1)} %get-tuple-element.8, f32[1024,128]{1,0:T(8,128)S(1)} %get-tuple-element.7), kind=kLoop, calls=%fused_computation | loop fusion | flops 262144 | bytes 2097152 | tf_op jit(solution)/shard_map/concatenate | solution.py:465

commit v3 on v2

--- a/solution.py
+++ b/solution.py
@@ -12,15 +12,16 @@
 MESH = pl.DeviceIdType.MESH
 
 
-def split_tiles(tiles, count):
-    per_owner = next(p for p in range(1, tiles + 1) if tiles % p == 0 and p * count >= tiles)
+def split_tiles(tiles, most):
+    per_owner = next(p for p in range(1, tiles + 1) if tiles % p == 0 and p * most >= tiles)
     return per_owner, tiles // per_owner
 
 
 class Sweep:
-    def __init__(self, axis, count, tiles, parts, refs):
+    def __init__(self, axis, count, most, tiles, parts, refs):
         self.axis, self.count, self.tiles = axis, count, tiles
-        self.per, self.owners = split_tiles(tiles, count)
+        self.per, self.owners = split_tiles(tiles, most)
+        self.base = (count - self.owners) // 2
         self.parts = parts if self.owners % parts == 0 else 1
         (self.t, self.rt, self.b, self.rb, self.s, self.rs, self.pe, self.up_sems, self.back_sems) = refs
         self.me = lax.axis_index(axis)
@@ -28,24 +29,24 @@
     def others(self):
         return [lax.rem(self.me + d, self.count) for d in range(1, self.count)]
 
+    def of(self, owner):
+        return pl.ds((owner - self.base) * self.per, self.per)
+
     def own(self):
-        return pl.ds(self.me * self.per, self.per)
+        return self.of(self.me)
+
+    def is_owner(self):
+        return jnp.logical_and(self.me >= self.base, self.me < self.base + self.owners)
 
     def bounds(self, part):
-        return self.owners * part // self.parts, self.owners * (part + 1) // self.parts
-
-    def within(self, index, low, high, body):
-        if low == 0 and high == self.count:
+        each = self.owners // self.parts
+        return self.base + each * part, self.base + each * (part + 1)
+
+    def on_owner(self, body):
+        if self.owners == self.count:
             body()
-        elif low == 0:
-            pl.when(index < high)(body)
-        elif high == self.count:
-            pl.when(index >= low)(body)
         else:
-            pl.when(jnp.logical_and(index >= low, index < high))(body)
-
-    def guarded(self, index, body):
-        self.within(index, 0, self.owners, body)
+            pl.when(self.is_owner())(body)
 
     def copy(self, src, dst, send_sem, recv_sem, target):
         return pltpu.make_async_remote_copy(
@@ -64,18 +65,16 @@
         return self.copy(src, dst, self.up_sems.at[kind, 0], self.up_sems.at[kind, 1], target)
 
     def send(self, kind, part=None):
-        low, high = (0, self.owners) if part is None else self.bounds(part)
+        low, high = (self.base, self.base + self.owners) if part is None else self.bounds(part)
         mine, there = self.buffers(kind)
-
-        def start(target):
-            self.up(kind, mine.at[pl.ds(target * self.per, self.per)], there.at[self.me], target).start()
-
-        def keep():
-            there[self.me] = mine[self.own()]
-
-        for target in self.others():
-            self.within(target, low, high, lambda target=target: start(target))
-        self.within(self.me, low, high, keep)
+        for owner in range(low, high):
+            @pl.when(self.me != owner)
+            def _(owner=owner):
+                self.up(kind, mine.at[self.of(owner)], there.at[self.me], owner).start()
+
+            @pl.when(self.me == owner)
+            def _(owner=owner):
+                there[owner] = mine[self.of(owner)]
 
     def arrived(self, kind):
         there = self.buffers(kind)[1].at[pl.ds(0, self.count - 1)]
@@ -92,13 +91,13 @@
                 resistance = (self.rt[j, :, 0] * resistance + self.rt[j, :, 1]) * inverse
             self.pe[self.count, :, 0] = resistance
 
-        self.guarded(self.me, body)
+        self.on_owner(body)
 
     def back(self, src, dst, part, target):
         return self.copy(src, dst, self.back_sems.at[0], self.back_sems.at[1 + part], target)
 
     def solve(self):
-        part = lax.div(self.me, self.owners // self.parts)
+        part = lax.div(self.me - self.base, self.owners // self.parts)
 
         def body():
             self.arrived(1)
@@ -117,7 +116,7 @@
                 self.back(self.s.at[target], self.rs.at[self.own()], part, target).start()
             self.rs[self.own()] = self.s[self.me]
 
-        self.guarded(self.me, body)
+        self.on_owner(body)
 
     def receive(self, part):
         if part >= self.parts:
@@ -145,9 +144,9 @@
             mine = self.s.at[pl.ds(0, self.count - 1)]
             self.back(mine, mine, 0, self.others()[0]).wait_send()
 
-        self.guarded(self.me, owner)
+        self.on_owner(owner)
         if self.owners < self.count:
-            pl.when(self.me >= self.owners)(lambda: sent(self.owners))
+            pl.when(jnp.logical_not(self.is_owner()))(lambda: sent(self.owners))
 
 
 def kernel(nx, ny, lx, ly, nh, pitch, *refs):
@@ -158,8 +157,8 @@
     x_refs, y_refs = refs[20:29], refs[29:38]
     rtx, rty = ly // ROWS, lx // ROWS
     mx, my = lax.axis_index("gx"), lax.axis_index("gy")
-    X = Sweep("gx", nx, nh * rtx, nh, x_refs)
-    Y = Sweep("gy", ny, nh * rty, nh, y_refs)
+    X = Sweep("gx", nx, max(1, nx // 2), nh * rtx, nh, x_refs)
+    Y = Sweep("gy", ny, ny, nh * rty, nh, y_refs)
 
     around = [(-1, 0), (1, 0), (0, -1), (0, 1), (-1, -1), (-1, 1), (1, -1), (1, 1)]
 
@@ -398,17 +397,25 @@
                 i = g * ROWS + r
                 x = x + RY[h, rows(i, lx), :] * j
                 j = (j - HT[h, rows(i, lx), :]) + x
-                out[h][pl.ds(i, lx, stride=ly), :] = x
+                HALF[h, pl.ds(i, lx, stride=pitch), :] = x
             return x, j
 
         start = (get_tiles(Y.rs, h, rty, 0), get_tiles(Y.rs, h, rty, 1))
         lax.fori_loop(0, ly // ROWS, steps, start)
 
+        def planes(g, carry, h=h):
+            for r in range(ROWS):
+                i = g * ROWS + r
+                out[h][rows(i, ly), :] = HALF[h, pl.ds(pl.multiple_of(i * pitch, ROWS), ly), :]
+            return carry
+
+        lax.fori_loop(0, lx // ROWS, planes, 0)
+
     Y.drain()
 
 
-def sweep_scratch(count, tiles, parts):
-    per, owners = split_tiles(tiles, count)
+def sweep_scratch(count, most, tiles, parts):
+    per, owners = split_tiles(tiles, most)
     return [
         pltpu.VMEM((tiles, 4, ROWS, LANES), jnp.float32),
         pltpu.VMEM((count, per, 4, ROWS, LANES), jnp.float32),
@@ -444,8 +451,8 @@
         pltpu.SemaphoreType.DMA((4, nh)),
         pltpu.SemaphoreType.DMA((8,)),
         pltpu.SemaphoreType.DMA((8,)),
-        *sweep_scratch(nx, nh * ly // ROWS, nh),
-        *sweep_scratch(ny, nh * lx // ROWS, nh),
+        *sweep_scratch(nx, max(1, nx // 2), nh * ly // ROWS, nh),
+        *sweep_scratch(ny, ny, nh * lx // ROWS, nh),
     ]
     result = pl.pallas_call(
         functools.partial(kernel, nx, ny, lx, ly, nh, pitch),
@@ -461,7 +468,6 @@
         ),
         name="adi_step",
     )(*flat)
-
     return jnp.concatenate(result, axis=1).reshape(lx, ly, nz)
 
 

time: 25.9 us -> 24.9 us (0.961)
  Pallas kernels: 24.8 us -> 23.7 us
    pallas_call x1, Pallas kernels: 24.8 us -> 23.7 us  [shards(): pl.pallas_call(functools.partial(kernel, nx, ny, lx, ly, nh, pitch), out_...]
where the time goes in v3:
time: 24.9 us; the launch traced here: 24.8 us
  Pallas kernels  23.7 us (95%)
  other arithmetic  1.04 us (4%)
    pallas_call x1, Pallas kernels, shards(): pl.pallas_call(functools.partial(kernel, nx, ny, lx, ly, nh, pitch), out_...  23.7 us
    concatenate x1, other arithmetic, shards(): return jnp.concatenate(result, axis=1).reshape(lx, ly, nz)  1.04 us

profile of v3, /device:TPU:0, one launch (start us, length us, event | category | flops | bytes accessed | tf_op | source)
XLA Modules:
  0.0 24.8 jit_solution(3570421291393940424)
XLA Ops:
  0.0 23.7 %adi_step.1 = (f32[1024,128]{1,0:T(8,128)S(1)}, f32[1024,128]{1,0:T(8,128)S(1)}) custom-call(f32[1024,256]{1,0:T(8,128)} %bitcast.5, f32[1024,256]{1,0:T(8,128)} %bitcast.6, f32[1024,256]{1,0:T(8,128)} %bitcast.7, f32[1024,256]{1,0:T(8,128)} %bitcast.8), custom_call_target="tpu_custom_call" | custom-call | flops 15728640 | bytes 5242880 | tf_op jit(solution)/shard_map/adi_step/pallas_call | solution.py:457
  23.7 1.0 %pad_maximum_fusion = f32[1024,256]{1,0:T(8,128)} fusion(f32[1024,128]{1,0:T(8,128)S(1)} %get-tuple-element.8, f32[1024,128]{1,0:T(8,128)S(1)} %get-tuple-element.7), kind=kLoop, calls=%fused_computation | loop fusion | flops 262144 | bytes 2097152 | tf_op jit(solution)/shard_map/concatenate | solution.py:471

commit v4 on v3

--- a/solution.py
+++ b/solution.py
@@ -195,13 +195,6 @@
 
     start(0)
     start(1)
-
-    for h in range(nh):
-        load(0, h).wait()
-    start(3)
-    for h in range(nh):
-        ys[0, h] = F[h, pl.ds(ly, lx, stride=ly), :]
-        ys[1, h] = F[h, pl.ds(ly + ly - 1, lx, stride=ly), :]
 
     def halo(k):
         dx, dy = around[k]
@@ -241,12 +234,22 @@
         )
 
     diagonal = sum(jnp.where(exists(dx, dy), 1, 0) for dx, dy in around[4:])
+
+    def send_halo(low, high):
+        for k in range(low, high):
+            @pl.when(exists(*around[k]))
+            def _(k=k):
+                halo(k).start()
+
+    for h in range(nh):
+        load(0, h).wait()
+    start(3)
     pl.semaphore_wait(barrier, nx - 1 + ny - 1 + diagonal)
-
-    for k, (dx, dy) in enumerate(around):
-        @pl.when(exists(dx, dy))
-        def _(k=k):
-            halo(k).start()
+    send_halo(0, 2)
+    for h in range(nh):
+        ys[0, h] = F[h, pl.ds(ly, lx, stride=ly), :]
+        ys[1, h] = F[h, pl.ds(ly + ly - 1, lx, stride=ly), :]
+    send_halo(2, 8)
 
     for k, (dx, dy) in enumerate(around):
         @pl.when(jnp.logical_not(exists(dx, dy)))
@@ -338,19 +341,22 @@
         send_part(X, h)
     X.prepare()
 
-    for h in range(nh):
+    def transfer_y(h):
         load(2, h).wait()
 
-        def resistance_y(i, h=h):
+        def resistance_y(i):
             rho = (1.0 / step_dt) / KY[h, pl.ds(i, lx, stride=ly), :]
             RY[h, rows(i, lx), :] = rho
             return rho
 
         put_tiles(Y.t, h, rty, transfer(ly, lx, resistance_y))
+
+    for h in range(nh // 2):
+        transfer_y(h)
+    X.solve()
+    for h in range(nh // 2, nh):
+        transfer_y(h)
     Y.send(0)
-
-    X.solve()
-    Y.prepare()
 
     for h in range(nh):
         X.receive(h)
@@ -386,6 +392,7 @@
         def _(k=k):
             halo(k).wait_send()
     X.drain()
+    Y.prepare()
     Y.solve()
 
     for h in range(nh):

time: 24.9 us -> 24.9 us (level)
  no operation moved by 1% of the time
where the time goes in v4:
time: 24.9 us; the launch traced here: 24.8 us
  Pallas kernels  23.8 us (96%)
  other arithmetic  1.04 us (4%)
    pallas_call x1, Pallas kernels, shards(): pl.pallas_call(functools.partial(kernel, nx, ny, lx, ly, nh, pitch), out_...  23.8 us
    concatenate x1, other arithmetic, shards(): return jnp.concatenate(result, axis=1).reshape(lx, ly, nz)  1.04 us

profile of v4, /device:TPU:0, one launch (start us, length us, event | category | flops | bytes accessed | tf_op | source)
XLA Modules:
  0.0 24.8 jit_solution(12899205996599788305)
XLA Ops:
  0.0 23.8 %adi_step.1 = (f32[1024,128]{1,0:T(8,128)S(1)}, f32[1024,128]{1,0:T(8,128)S(1)}) custom-call(f32[1024,256]{1,0:T(8,128)} %bitcast.5, f32[1024,256]{1,0:T(8,128)} %bitcast.6, f32[1024,256]{1,0:T(8,128)} %bitcast.7, f32[1024,256]{1,0:T(8,128)} %bitcast.8), custom_call_target="tpu_custom_call" | custom-call | flops 15728640 | bytes 5242880 | tf_op jit(solution)/shard_map/adi_step/pallas_call | solution.py:464
  23.8 1.0 %pad_maximum_fusion = f32[1024,256]{1,0:T(8,128)} fusion(f32[1024,128]{1,0:T(8,128)S(1)} %get-tuple-element.8, f32[1024,128]{1,0:T(8,128)S(1)} %get-tuple-element.7), kind=kLoop, calls=%fused_computation | loop fusion | flops 262144 | bytes 2097152 | tf_op jit(solution)/shard_map/concatenate | solution.py:478

commit v5 on v4

--- a/solution.py
+++ b/solution.py
@@ -149,16 +149,84 @@
             pl.when(jnp.logical_not(self.is_owner()))(lambda: sent(self.owners))
 
 
+class Gathered:
+    def __init__(self, axis, count, tiles, parts, refs):
+        self.axis, self.count, self.parts = axis, count, parts
+        self.tiles = tiles // parts
+        (self.t, self.rt, self.b, self.rb, self.s, self.pe, self.send_sems, self.recv_sems) = refs
+        self.me = lax.axis_index(axis)
+
+    def others(self):
+        return [lax.rem(self.me + d, self.count) for d in range(1, self.count)]
+
+    def copy(self, src, dst, send, recv, target):
+        return pltpu.make_async_remote_copy(
+            src_ref=src,
+            dst_ref=dst,
+            send_sem=self.send_sems.at[send],
+            recv_sem=self.recv_sems.at[recv],
+            device_id={self.axis: target},
+            device_id_type=MESH,
+        )
+
+    def send_matrices(self):
+        for target in self.others():
+            self.copy(self.t, self.rt.at[self.me], 0, 0, target).start()
+        self.rt[self.me] = self.t[...]
+
+    def send(self, part):
+        for target in self.others():
+            self.copy(self.b.at[part], self.rb.at[part, self.me], 1, 1 + part, target).start()
+        self.rb[part, self.me] = self.b[part]
+
+    def prepare(self):
+        there = self.rt.at[pl.ds(0, self.count - 1)]
+        self.copy(there, there, 0, 0, self.others()[0]).wait_recv()
+        for part in range(self.parts):
+            resistance = jnp.zeros((self.tiles, ROWS, LANES), jnp.float32)
+            for j in range(self.count):
+                through, shunt, last = (self.rt[j, part, :, c] for c in range(3))
+                inverse = 1.0 / (shunt * resistance + last)
+                self.pe[j, part, 0] = resistance
+                self.pe[j, part, 1] = inverse
+                resistance = (resistance * inverse + through) / last
+            self.pe[self.count, part, 0] = resistance
+
+    def solve(self, part):
+        there = self.rb.at[part, pl.ds(0, self.count - 1)]
+        self.copy(there, there, 1, 1 + part, self.others()[0]).wait_recv()
+        offset = jnp.zeros((self.tiles, ROWS, LANES), jnp.float32)
+        offsets = []
+        for j in range(self.count):
+            offsets.append(offset)
+            value, flux = self.rb[part, j, :, 0], self.rb[part, j, :, 1]
+            offset = offset * self.pe[j, part, 1] + (value - self.pe[j + 1, part, 0] * flux)
+        flux = jnp.zeros((self.tiles, ROWS, LANES), jnp.float32)
+        for j in reversed(range(self.count)):
+            share = self.rt[j, part, :, 1] * offsets[j] + self.rb[part, j, :, 1]
+            flux = (flux - share) * self.pe[j, part, 1]
+            self.s[j, 0] = self.pe[j, part, 0] * flux + offsets[j]
+            self.s[j, 1] = flux
+        state = self.s[self.me]
+        return [state[c].reshape(self.tiles * ROWS, LANES) for c in range(2)]
+
+    def drain(self):
+        mine = self.rt.at[pl.ds(0, self.count - 1)]
+        self.copy(mine, mine, 0, 0, self.others()[0]).wait_send()
+        mine = self.rb.at[:, pl.ds(0, self.count - 1)]
+        self.copy(mine, mine, 1, 1, self.others()[0]).wait_send()
+
+
 def kernel(nx, ny, lx, ly, nh, pitch, *refs):
     field, cond_x, cond_y, weight = refs[:4]
     out, refs = refs[4:4 + nh], refs[4 + nh - 5:]
     F, KX, KY, R, RY, HALF, HT, xh, ys, yh, ch, dl = refs[5:17]
     in_sem, halo_send, halo_recv = refs[17:20]
-    x_refs, y_refs = refs[20:29], refs[29:38]
+    x_refs, y_refs = refs[20:29], refs[29:37]
     rtx, rty = ly // ROWS, lx // ROWS
     mx, my = lax.axis_index("gx"), lax.axis_index("gy")
     X = Sweep("gx", nx, max(1, nx // 2), nh * rtx, nh, x_refs)
-    Y = Sweep("gy", ny, ny, nh * rty, nh, y_refs)
+    Y = Gathered("gy", ny, nh * rty, nh, y_refs)
 
     around = [(-1, 0), (1, 0), (0, -1), (0, 1), (-1, -1), (-1, 1), (1, -1), (1, 1)]
 
@@ -349,14 +417,15 @@
             RY[h, rows(i, lx), :] = rho
             return rho
 
-        put_tiles(Y.t, h, rty, transfer(ly, lx, resistance_y))
+        _, through, shunt, last = transfer(ly, lx, resistance_y)
+        put_tiles(Y.t.at[h], 0, rty, (through, shunt, last))
 
     for h in range(nh // 2):
         transfer_y(h)
     X.solve()
     for h in range(nh // 2, nh):
         transfer_y(h)
-    Y.send(0)
+    Y.send_matrices()
 
     for h in range(nh):
         X.receive(h)
@@ -384,8 +453,8 @@
             return x, j
 
         zero = jnp.zeros((lx, LANES), jnp.float32)
-        put_tiles(Y.b, h, rty, lax.fori_loop(0, ly // ROWS, steps_y, (zero, zero)))
-        send_part(Y, h)
+        put_tiles(Y.b.at[h], 0, rty, lax.fori_loop(0, ly // ROWS, steps_y, (zero, zero)))
+        Y.send(h)
 
     for k, (dx, dy) in enumerate(around):
         @pl.when(exists(dx, dy))
@@ -393,10 +462,9 @@
             halo(k).wait_send()
     X.drain()
     Y.prepare()
-    Y.solve()
-
-    for h in range(nh):
-        Y.receive(h)
+
+    for h in range(nh):
+        start = Y.solve(h)
 
         def steps(g, carry, h=h):
             x, j = carry
@@ -407,8 +475,7 @@
                 HALF[h, pl.ds(i, lx, stride=pitch), :] = x
             return x, j
 
-        start = (get_tiles(Y.rs, h, rty, 0), get_tiles(Y.rs, h, rty, 1))
-        lax.fori_loop(0, ly // ROWS, steps, start)
+        lax.fori_loop(0, ly // ROWS, steps, tuple(start))
 
         def planes(g, carry, h=h):
             for r in range(ROWS):
@@ -432,6 +499,20 @@
         pltpu.VMEM((tiles, 2, ROWS, LANES), jnp.float32),
         pltpu.VMEM((count + 1, per, 2, ROWS, LANES), jnp.float32),
         pltpu.SemaphoreType.DMA((2, 2)),
+        pltpu.SemaphoreType.DMA((1 + parts,)),
+    ]
+
+
+def gathered_scratch(count, tiles, parts):
+    each = tiles // parts
+    return [
+        pltpu.VMEM((parts, each, 3, ROWS, LANES), jnp.float32),
+        pltpu.VMEM((count, parts, each, 3, ROWS, LANES), jnp.float32),
+        pltpu.VMEM((parts, each, 2, ROWS, LANES), jnp.float32),
+        pltpu.VMEM((parts, count, each, 2, ROWS, LANES), jnp.float32),
+        pltpu.VMEM((count, 2, each, ROWS, LANES), jnp.float32),
+        pltpu.VMEM((count + 1, parts, 2, each, ROWS, LANES), jnp.float32),
+        pltpu.SemaphoreType.DMA((2,)),
         pltpu.SemaphoreType.DMA((1 + parts,)),
     ]
 
@@ -459,7 +540,7 @@
         pltpu.SemaphoreType.DMA((8,)),
         pltpu.SemaphoreType.DMA((8,)),
         *sweep_scratch(nx, max(1, nx // 2), nh * ly // ROWS, nh),
-        *sweep_scratch(ny, ny, nh * lx // ROWS, nh),
+        *gathered_scratch(ny, nh * lx // ROWS, nh),
     ]
     result = pl.pallas_call(
         functools.partial(kernel, nx, ny, lx, ly, nh, pitch),

time: 24.9 us -> 22.7 us (0.912)
  Pallas kernels: 23.8 us -> 21.5 us
    pallas_call x1, Pallas kernels: 23.8 us -> 21.5 us  [shards(): pl.pallas_call(functools.partial(kernel, nx, ny, lx, ly, nh, pitch), out_...]
where the time goes in v5:
time: 22.7 us; the launch traced here: 22.6 us
  Pallas kernels  21.5 us (95%)
  other arithmetic  1.04 us (5%)
    pallas_call x1, Pallas kernels, shards(): pl.pallas_call(functools.partial(kernel, nx, ny, lx, ly, nh, pitch), out_...  21.5 us
    concatenate x1, other arithmetic, shards(): return jnp.concatenate(result, axis=1).reshape(lx, ly, nz)  1.04 us

profile of v5, /device:TPU:0, one launch (start us, length us, event | category | flops | bytes accessed | tf_op | source)
XLA Modules:
  0.0 22.6 jit_solution(2525816833202291831)
XLA Ops:
  0.0 21.5 %adi_step.1 = (f32[1024,128]{1,0:T(8,128)S(1)}, f32[1024,128]{1,0:T(8,128)S(1)}) custom-call(f32[1024,256]{1,0:T(8,128)} %bitcast.5, f32[1024,256]{1,0:T(8,128)} %bitcast.6, f32[1024,256]{1,0:T(8,128)} %bitcast.7, f32[1024,256]{1,0:T(8,128)} %bitcast.8), custom_call_target="tpu_custom_call" | custom-call | flops 15728640 | bytes 5242880 | tf_op jit(solution)/shard_map/adi_step/pallas_call | solution.py:545
  21.5 1.0 %pad_maximum_fusion = f32[1024,256]{1,0:T(8,128)} fusion(f32[1024,128]{1,0:T(8,128)S(1)} %get-tuple-element.8, f32[1024,128]{1,0:T(8,128)S(1)} %get-tuple-element.7), kind=kLoop, calls=%fused_computation | loop fusion | flops 262144 | bytes 2097152 | tf_op jit(solution)/shard_map/concatenate | solution.py:559

commit v6 on v5

--- a/solution.py
+++ b/solution.py
@@ -153,7 +153,7 @@
     def __init__(self, axis, count, tiles, parts, refs):
         self.axis, self.count, self.parts = axis, count, parts
         self.tiles = tiles // parts
-        (self.t, self.rt, self.b, self.rb, self.s, self.pe, self.send_sems, self.recv_sems) = refs
+        (self.t, self.rt, self.b, self.rb, self.w, self.pe, self.send_sems, self.recv_sems) = refs
         self.me = lax.axis_index(axis)
 
     def others(self):
@@ -169,49 +169,56 @@
             device_id_type=MESH,
         )
 
-    def send_matrices(self):
+    def send_matrices(self, part):
         for target in self.others():
-            self.copy(self.t, self.rt.at[self.me], 0, 0, target).start()
-        self.rt[self.me] = self.t[...]
+            self.copy(self.t.at[part], self.rt.at[part, self.me], 0, part, target).start()
+        self.rt[part, self.me] = self.t[part]
+
+    def prepare(self, part):
+        there = self.rt.at[part, pl.ds(0, self.count - 1)]
+        self.copy(there, there, 0, part, self.others()[0]).wait_recv()
+        low = jnp.zeros((self.tiles, ROWS, LANES), jnp.float32)
+        for j in range(self.count):
+            through, shunt, last = (self.rt[part, j, :, c] for c in range(3))
+            inverse = 1.0 / (shunt * low + last)
+            self.pe[part, j, 0] = low
+            self.pe[part, j, 1] = inverse
+            low = (low * inverse + through) / last
+        self.pe[part, self.count, 0] = low
+        high = jnp.zeros((self.tiles, ROWS, LANES), jnp.float32)
+        for j in reversed(range(self.count)):
+            through, shunt, last = (self.rt[part, j, :, c] for c in range(3))
+            inverse = 1.0 / (last + high * through)
+            self.pe[part, j + 1, 2] = high
+            self.pe[part, j, 3] = inverse
+            high = (high * inverse + shunt) / last
+        self.pe[part, 0, 2] = high
 
     def send(self, part):
+        value, flux = self.b[part, :, 0], self.b[part, :, 1]
+        self.w[part, 0] = value - self.pe[part, self.me + 1, 0] * flux
+        self.w[part, 1] = flux + self.pe[part, self.me + 1, 2] * value
         for target in self.others():
-            self.copy(self.b.at[part], self.rb.at[part, self.me], 1, 1 + part, target).start()
-        self.rb[part, self.me] = self.b[part]
-
-    def prepare(self):
-        there = self.rt.at[pl.ds(0, self.count - 1)]
-        self.copy(there, there, 0, 0, self.others()[0]).wait_recv()
-        for part in range(self.parts):
-            resistance = jnp.zeros((self.tiles, ROWS, LANES), jnp.float32)
-            for j in range(self.count):
-                through, shunt, last = (self.rt[j, part, :, c] for c in range(3))
-                inverse = 1.0 / (shunt * resistance + last)
-                self.pe[j, part, 0] = resistance
-                self.pe[j, part, 1] = inverse
-                resistance = (resistance * inverse + through) / last
-            self.pe[self.count, part, 0] = resistance
+            side = jnp.where(target > self.me, 0, 1)
+            self.copy(self.w.at[part, side], self.rb.at[part, self.me], 1, self.parts + part, target).start()
+        self.rb[part, self.me] = self.w[part, 1]
 
     def solve(self, part):
         there = self.rb.at[part, pl.ds(0, self.count - 1)]
-        self.copy(there, there, 1, 1 + part, self.others()[0]).wait_recv()
+        self.copy(there, there, 1, self.parts + part, self.others()[0]).wait_recv()
         offset = jnp.zeros((self.tiles, ROWS, LANES), jnp.float32)
-        offsets = []
-        for j in range(self.count):
-            offsets.append(offset)
-            value, flux = self.rb[part, j, :, 0], self.rb[part, j, :, 1]
-            offset = offset * self.pe[j, part, 1] + (value - self.pe[j + 1, part, 0] * flux)
-        flux = jnp.zeros((self.tiles, ROWS, LANES), jnp.float32)
+        for j in range(self.count - 1):
+            offset = jnp.where(j < self.me, offset * self.pe[part, j, 1] + self.rb[part, j], offset)
+        push = jnp.zeros((self.tiles, ROWS, LANES), jnp.float32)
         for j in reversed(range(self.count)):
-            share = self.rt[j, part, :, 1] * offsets[j] + self.rb[part, j, :, 1]
-            flux = (flux - share) * self.pe[j, part, 1]
-            self.s[j, 0] = self.pe[j, part, 0] * flux + offsets[j]
-            self.s[j, 1] = flux
-        state = self.s[self.me]
-        return [state[c].reshape(self.tiles * ROWS, LANES) for c in range(2)]
+            push = jnp.where(j >= self.me, (push - self.rb[part, j]) * self.pe[part, j, 3], push)
+        low, high = self.pe[part, self.me, 0], self.pe[part, self.me, 2]
+        flux = (push - high * offset) / (1.0 + high * low)
+        state = (low * flux + offset, flux)
+        return [value.reshape(self.tiles * ROWS, LANES) for value in state]
 
     def drain(self):
-        mine = self.rt.at[pl.ds(0, self.count - 1)]
+        mine = self.rt.at[:, pl.ds(0, self.count - 1)]
         self.copy(mine, mine, 0, 0, self.others()[0]).wait_send()
         mine = self.rb.at[:, pl.ds(0, self.count - 1)]
         self.copy(mine, mine, 1, 1, self.others()[0]).wait_send()
@@ -420,14 +427,13 @@
         _, through, shunt, last = transfer(ly, lx, resistance_y)
         put_tiles(Y.t.at[h], 0, rty, (through, shunt, last))
 
-    for h in range(nh // 2):
+    for h in range(nh):
         transfer_y(h)
+        Y.send_matrices(h)
     X.solve()
-    for h in range(nh // 2, nh):
-        transfer_y(h)
-    Y.send_matrices()
-
-    for h in range(nh):
+
+    for h in range(nh):
+        Y.prepare(h)
         X.receive(h)
 
         def steps(g, carry, h=h):
@@ -461,7 +467,6 @@
         def _(k=k):
             halo(k).wait_send()
     X.drain()
-    Y.prepare()
 
     for h in range(nh):
         start = Y.solve(h)
@@ -507,13 +512,13 @@
     each = tiles // parts
     return [
         pltpu.VMEM((parts, each, 3, ROWS, LANES), jnp.float32),
-        pltpu.VMEM((count, parts, each, 3, ROWS, LANES), jnp.float32),
+        pltpu.VMEM((parts, count, each, 3, ROWS, LANES), jnp.float32),
         pltpu.VMEM((parts, each, 2, ROWS, LANES), jnp.float32),
-        pltpu.VMEM((parts, count, each, 2, ROWS, LANES), jnp.float32),
-        pltpu.VMEM((count, 2, each, ROWS, LANES), jnp.float32),
-        pltpu.VMEM((count + 1, parts, 2, each, ROWS, LANES), jnp.float32),
+        pltpu.VMEM((parts, count, each, ROWS, LANES), jnp.float32),
+        pltpu.VMEM((parts, 2, each, ROWS, LANES), jnp.float32),
+        pltpu.VMEM((parts, count + 1, 4, each, ROWS, LANES), jnp.float32),
         pltpu.SemaphoreType.DMA((2,)),
-        pltpu.SemaphoreType.DMA((1 + parts,)),
+        pltpu.SemaphoreType.DMA((2 * parts,)),
     ]
 
 

time: 22.7 us -> 22.3 us (0.982)
  Pallas kernels: 21.5 us -> 21.1 us
    pallas_call x1, Pallas kernels: 21.5 us -> 21.1 us  [shards(): pl.pallas_call(functools.partial(kernel, nx, ny, lx, ly, nh, pitch), out_...]
where the time goes in v6:
time: 22.3 us; the launch traced here: 22.2 us
  Pallas kernels  21.1 us (95%)
  other arithmetic  1.04 us (5%)
    pallas_call x1, Pallas kernels, shards(): pl.pallas_call(functools.partial(kernel, nx, ny, lx, ly, nh, pitch), out_...  21.1 us
    concatenate x1, other arithmetic, shards(): return jnp.concatenate(result, axis=1).reshape(lx, ly, nz)  1.04 us

profile of v6, /device:TPU:0, one launch (start us, length us, event | category | flops | bytes accessed | tf_op | source)
XLA Modules:
  0.0 22.2 jit_solution(14420862227220321058)
XLA Ops:
  0.0 21.1 %adi_step.1 = (f32[1024,128]{1,0:T(8,128)S(1)}, f32[1024,128]{1,0:T(8,128)S(1)}) custom-call(f32[1024,256]{1,0:T(8,128)} %bitcast.5, f32[1024,256]{1,0:T(8,128)} %bitcast.6, f32[1024,256]{1,0:T(8,128)} %bitcast.7, f32[1024,256]{1,0:T(8,128)} %bitcast.8), custom_call_target="tpu_custom_call" | custom-call | flops 15728640 | bytes 5242880 | tf_op jit(solution)/shard_map/adi_step/pallas_call | solution.py:550
  21.1 1.0 %pad_maximum_fusion = f32[1024,256]{1,0:T(8,128)} fusion(f32[1024,128]{1,0:T(8,128)S(1)} %get-tuple-element.8, f32[1024,128]{1,0:T(8,128)S(1)} %get-tuple-element.7), kind=kLoop, calls=%fused_computation | loop fusion | flops 262144 | bytes 2097152 | tf_op jit(solution)/shard_map/concatenate | solution.py:564
